TPU v7x, 256 devices: a whole 4x4x8 slice. The times are simulated.
256 devices in a mesh: grp: 8 (over y_lo, x), seq: 32 (over z, y_hi, core).
Axes of the slice: x: 4, y: 4 (y_hi: 2, y_lo: 2; y = y_hi * 2 + y_lo), z: 8, core: 2. Of those that a mesh axis runs over, the one named last changes fastest.
Arguments:
- fake_tokens: bfloat16 [8, 6144, 1536], P('grp', 'seq'), may hold values from -16 to 16
- real_tokens: bfloat16 [8, 6144, 1536], P('grp', 'seq'), may hold values from -6 to 6
- proj_weight: bfloat16 [1536, 2048], P('seq'), may hold values from -0.15625 to 0.15625
- score_vector: float32 [2048], replicated, may hold values from -0.25 to 0.25
Outputs:
- grad_weight: float32 [1536, 2048], P('seq')
All inputs are finite; a program needn't handle non-finite values.
Results may differ from a plain program's by a relative error of at most 0.0003.
Values may be sent and summed in bfloat16 or wider, within the bound.
No kernel may reach another device: no remote copies, remote signals or barrier semaphores. Data moves between devices by JAX's collectives and lax.ppermute only.
A program may use at most 64 MiB of HBM per device.

v0:
```python
import math
import jax
import jax.numpy as jnp
from jax import lax
from jax.sharding import PartitionSpec as P

R1_WEIGHT = 40.0


def per_device(fake_tokens, real_tokens, proj_weight, score_vector):
    fake_rows = fake_tokens[0]
    real_rows = real_tokens[0]
    tok_count = fake_rows.shape[0]
    hid_width = proj_weight.shape[1]
    loss_scale = math.sqrt(hid_width / (lax.axis_size("grp") * lax.axis_size("seq") * tok_count))
    joined = jnp.concatenate([fake_rows, real_rows], 0)
    shard_rows = lax.all_gather(proj_weight, "seq", axis=0, tiled=True)
    partial_pre = jnp.dot(joined, shard_rows, preferred_element_type=jnp.float32)
    full_weight = shard_rows
    preact, full_weight = (partial_pre, full_weight)
    squash = jax.nn.sigmoid(preact)
    slopes = squash * (1.0 + preact * (1.0 - squash))
    curves = squash * (1.0 - squash) * (2.0 + preact * (1.0 - 2.0 * squash))
    logits = jnp.dot(preact * squash, score_vector, precision=lax.Precision.HIGHEST)
    slopes_real = slopes[tok_count:]
    lifted = (slopes_real * score_vector).astype(jnp.bfloat16)
    input_grad = lax.dot_general(
        lifted, full_weight, (((1,), (1,)), ((), ())), preferred_element_type=jnp.float32
    )
    r1_cot = (loss_scale * R1_WEIGHT * input_grad).astype(jnp.bfloat16)
    back_grad = jnp.dot(r1_cot, full_weight, preferred_element_type=jnp.float32)
    fake_cot = (
        loss_scale * jax.nn.sigmoid(logits[:tok_count])[:, None] * slopes[:tok_count] * score_vector
    ).astype(jnp.bfloat16)
    real_cot = (
        -loss_scale * jax.nn.sigmoid(-logits[tok_count:])[:, None] * slopes_real * score_vector
        + back_grad * score_vector * curves[tok_count:]
    ).astype(jnp.bfloat16)
    left_rows = jnp.concatenate([fake_rows, real_rows, r1_cot], 0)
    right_rows = jnp.concatenate([fake_cot, real_cot, lifted], 0)
    grad_term = lax.dot_general(
        left_rows, right_rows, (((0,), (0,)), ((), ())), preferred_element_type=jnp.float32
    )
    grad_shard = lax.psum_scatter(grad_term, "seq", scatter_dimension=0, tiled=True)
    return lax.psum(grad_shard, "grp")


def solution(mesh):
    in_specs = (P("grp", "seq", None), P("grp", "seq", None), P("seq", None), P())
    out_specs = P("seq", None)
    return jax.shard_map(
        per_device, mesh=mesh, in_specs=in_specs, out_specs=out_specs, check_vma=False
    )
```

profile of v0, /device:TPU:32, one launch (start us, length us, event | category | flops | bytes accessed | tf_op | source)
XLA Modules:
  0.0 387.8 jit_solution(6854587875983400413)
XLA Ops:
  6.5 0.0 all-gather.2.cloned.1.call-start
  6.5 0.7 all-gather.2.cloned.1.call-update
  7.3 0.0 reduce-scatter.2.cloned.1.call-start
  7.3 99.7 %all-gather.2.cloned.1.call-done = bf16[1536,2048]{1,0:T(8,128)(2,1)} async-done(((bf16[48,2048]{1,0:T(8,128)(2,1)}), bf16[1536,2048]{1,0:T(8,128)(2,1)}) %all-gather.2.cloned.1.call-update) | async-done | bytes 6291472 | tf_op jit(solution)/shard_map/all_gather | solution.py:17
  107.0 0.0 copy-start
  107.0 5.6 %add_divide_fusion = (f32[384,2048]{1,0:T(8,128)S(1)}, f32[384,2048]{1,0:T(8,128)S(1)}, f32[384,2048]{1,0:T(8,128)S(1)}, f32[384,2048]{1,0:T(8,128)S(1)}) fusion(bf16[1536,2048]{1,0:T(8,128)(2,1)} %all-gather.2.cloned.1.call-done, bf16[192,1536]{1,0:T(8,128)(2,1)} %bitcast.12, bf16[192,1536]{1,0:T(8,128)(2,1)} %bitcast.14), kind=kOutput, calls=%fused_computation.3 | convolution fusion | flops 2423783424 | bytes 20054016 | tf_op jit(solution)/shard_map/dot_general | solution.py:18
  112.6 0.0 slice-start
  112.6 0.0 copy-done
  112.6 0.0 slice-start.1
  112.6 3.3 fusion.25
  115.9 0.1 divide_multiply_fusion.1
  116.0 0.3 fusion.20
  116.3 0.0 slice-done
  116.3 0.0 slice-done.1
  116.3 2.2 fusion.5
  118.6 0.0 copy-start.1
  118.6 0.0 copy-start.2
  118.6 1.8 fusion.4
  120.4 0.0 copy-done.1
  120.4 0.0 copy-done.2
  120.4 8.0 %fusion.6 = f32[1536,2048]{1,0:T(8,128)} fusion(bf16[192,2048]{1,0:T(8,128)(2,1)S(1)} %get-tuple-element.6, bf16[192,2048]{1,0:T(8,128)(2,1)S(1)} %fusion.4, bf16[192,2048]{1,0:T(8,128)(2,1)S(1)} %get-tuple-element.5, bf16[192,1536]{1,0:T(8,128)(2,1)S(1)} %fusion.5, bf16[192,1536]{1,0:T(8,128)(2,1)S(1)} %bitcast.13, bf16[192,1536]{1,0:T(8,128)(2,1)S(1)} %bitcast.15), kind=kOutput, calls=%fused_computation.10 | convolution fusion | flops 3636264960 | bytes 16711680 | tf_op jit(solution)/shard_map/dot_general | solution.py:41
  128.4 0.0 reduce-scatter.2.cloned.1.call-update
  128.5 0.0 all-reduce.2.cloned.1.call-start
  128.5 169.6 %reduce-scatter.2.cloned.1.call-done = f32[48,2048]{1,0:T(8,128)} async-done(((f32[1536,2048]{1,0:T(8,128)}), f32[48,2048]{1,0:T(8,128)}) %reduce-scatter.2.cloned.1.call-update) | async-done | bytes 393232 | tf_op jit(solution)/shard_map/reduce_scatter | solution.py:44
  298.1 0.0 all-reduce.2.cloned.1.call-update
  298.1 81.3 %all-reduce.2.cloned.1.call-done = f32[48,2048]{1,0:T(8,128)} async-done(((f32[48,2048]{1,0:T(8,128)}), f32[48,2048]{1,0:T(8,128)}) %all-reduce.2.cloned.1.call-update) | async-done | bytes 393232 | tf_op jit(solution)/shard_map/psum | solution.py:45
  379.5 1.8 copy.6
  (1 shorter events, 0.0 us)
Async XLA Ops:
  6.5 100.4 %all-gather.2.cloned.1.call-start = ((), (), s32[]{:S(2)}) async-start(), calls=%async_computation.1 | async-start | bytes 6488064 | tf_op jit(solution)/shard_map/all_gather | solution.py:17
  7.3 290.9 %reduce-scatter.2.cloned.1.call-start = ((), (), s32[]{:S(2)}) async-start(), calls=%async_computation.2 | async-start | bytes 12976128 | tf_op jit(solution)/shard_map/reduce_scatter | solution.py:44
  107.0 5.6 %copy-start = (f32[2048]{0:T(1024)S(1)}, f32[2048]{0:T(1024)}, u32[]{:S(2)}) copy-start(f32[2048]{0:T(1024)} %param.7) | copy-start | bytes 24580
  112.6 3.7 slice-start
  112.6 3.7 slice-start.1
  118.6 1.9 copy-start.1
  118.6 1.9 copy-start.2
  128.5 251.0 %all-reduce.2.cloned.1.call-start = ((), (), s32[]{:S(2)}) async-start(), calls=%async_computation.3 | async-start | bytes 786432 | tf_op jit(solution)/shard_map/psum | solution.py:45
Sparse Core Ops, SparseCore 0:
  10.1 96.7 all-gather.1
  128.6 169.4 reduce-scatter.1
  300.7 78.6 all-reduce.1
where the time goes:
time: 388 us
  waiting for transfers between devices  351 us (90%)
  matrix products  20.9 us (5%)
  between operations  13.2 us (3%)
    reduce_scatter x1, waiting for transfers between devices, per_device(): lax.psum_scatter(grad_term, 'seq', scatter_dimension=0, tiled=True)  170 us
    all_gather x1, waiting for transfers between devices, per_device(): shard_rows = lax.all_gather(proj_weight, 'seq', axis=0, tiled=True)  99.7 us
    psum x1, waiting for transfers between devices, per_device(): return lax.psum(grad_shard, 'grp')  81.3 us
    dot_general x1, matrix products, per_device(): lax.dot_general(left_rows, right_rows, (((0,), (0,)), ((), ())), preferre...  8.01 us
  transfers between devices with their start and end apart: 3, of which 3 were waited for; matrix products, arithmetic and copies ran while one was open for 0% of the time, Pallas kernels for 0%

commit v1 on v0

--- a/solution.py
+++ b/solution.py
@@ -5,6 +5,11 @@
 from jax.sharding import PartitionSpec as P
 
 R1_WEIGHT = 40.0
+
+
+def gather_and_add(block, axis):
+    pieces = lax.all_gather(block, axis)
+    return jnp.sum(pieces, axis=0)
 
 
 def per_device(fake_tokens, real_tokens, proj_weight, score_vector):
@@ -42,7 +47,7 @@
         left_rows, right_rows, (((0,), (0,)), ((), ())), preferred_element_type=jnp.float32
     )
     grad_shard = lax.psum_scatter(grad_term, "seq", scatter_dimension=0, tiled=True)
-    return lax.psum(grad_shard, "grp")
+    return gather_and_add(grad_shard, "grp")
 
 
 def solution(mesh):

time: 388 us -> 355 us (0.915)
  waiting for transfers between devices: 351 us -> 318 us
    psum x1 -> x0, waiting for transfers between devices: 81.3 us -> none  [per_device(): return lax.psum(grad_shard, 'grp')]
    all_gather x0 -> x1, waiting for transfers between devices: none -> 47.6 us  [gather_and_add(): pieces = lax.all_gather(block, axis)]
where the time goes in v1:
time: 355 us
  waiting for transfers between devices  318 us (90%)
  matrix products  20.9 us (6%)
  between operations  13.2 us (4%)
    reduce_scatter x1, waiting for transfers between devices, per_device(): lax.psum_scatter(grad_term, 'seq', scatter_dimension=0, tiled=True)  170 us
    all_gather x1, waiting for transfers between devices, per_device(): shard_rows = lax.all_gather(proj_weight, 'seq', axis=0, tiled=True)  99.7 us
    all_gather x1, waiting for transfers between devices, gather_and_add(): pieces = lax.all_gather(block, axis)  47.6 us
    dot_general x1, matrix products, per_device(): lax.dot_general(left_rows, right_rows, (((0,), (0,)), ((), ())), preferre...  8.01 us
  transfers between devices with their start and end apart: 3, of which 3 were waited for; matrix products, arithmetic and copies ran while one was open for 0% of the time, Pallas kernels for 0%

profile of v1, /device:TPU:32, one launch (start us, length us, event | category | flops | bytes accessed | tf_op | source)
XLA Modules:
  0.0 355.1 jit_solution(12180093741783458351)
XLA Ops:
  6.5 0.0 all-gather.4.cloned.1.call-start
  6.5 0.7 all-gather.4.cloned.1.call-update
  7.3 0.0 reduce-scatter.2.cloned.1.call-start
  7.3 99.7 %all-gather.4.cloned.1.call-done = bf16[1536,2048]{1,0:T(8,128)(2,1)} async-done(((bf16[48,2048]{1,0:T(8,128)(2,1)}), bf16[1536,2048]{1,0:T(8,128)(2,1)}) %all-gather.4.cloned.1.call-update) | async-done | bytes 6291472 | tf_op jit(solution)/shard_map/all_gather | solution.py:22
  107.0 0.0 copy-start
  107.0 5.6 %add_divide_fusion = (f32[384,2048]{1,0:T(8,128)S(1)}, f32[384,2048]{1,0:T(8,128)S(1)}, f32[384,2048]{1,0:T(8,128)S(1)}, f32[384,2048]{1,0:T(8,128)S(1)}) fusion(bf16[1536,2048]{1,0:T(8,128)(2,1)} %all-gather.4.cloned.1.call-done, bf16[192,1536]{1,0:T(8,128)(2,1)} %bitcast.14, bf16[192,1536]{1,0:T(8,128)(2,1)} %bitcast.16), kind=kOutput, calls=%fused_computation.3 | convolution fusion | flops 2423783424 | bytes 20054016 | tf_op jit(solution)/shard_map/dot_general | solution.py:23
  112.6 0.0 slice-start
  112.6 0.0 copy-done
  112.6 0.0 slice-start.1
  112.6 3.3 fusion.25
  115.9 0.1 divide_multiply_fusion.1
  116.0 0.3 fusion.20
  116.3 0.0 slice-done
  116.3 0.0 slice-done.1
  116.3 2.2 fusion.5
  118.6 0.0 copy-start.1
  118.6 0.0 copy-start.2
  118.6 1.8 fusion.4
  120.4 0.0 copy-done.1
  120.4 0.0 copy-done.2
  120.4 8.0 %fusion.6 = f32[1536,2048]{1,0:T(8,128)} fusion(bf16[192,2048]{1,0:T(8,128)(2,1)S(1)} %get-tuple-element.6, bf16[192,2048]{1,0:T(8,128)(2,1)S(1)} %fusion.4, bf16[192,2048]{1,0:T(8,128)(2,1)S(1)} %get-tuple-element.5, bf16[192,1536]{1,0:T(8,128)(2,1)S(1)} %fusion.5, bf16[192,1536]{1,0:T(8,128)(2,1)S(1)} %bitcast.15, bf16[192,1536]{1,0:T(8,128)(2,1)S(1)} %bitcast.17), kind=kOutput, calls=%fused_computation.10 | convolution fusion | flops 3636264960 | bytes 16711680 | tf_op jit(solution)/shard_map/dot_general | solution.py:46
  128.4 0.0 reduce-scatter.2.cloned.1.call-update
  128.5 0.0 all-gather.6.cloned.1.call-start
  128.5 169.6 %reduce-scatter.2.cloned.1.call-done = f32[48,2048]{1,0:T(8,128)} async-done(((f32[1536,2048]{1,0:T(8,128)}), f32[48,2048]{1,0:T(8,128)}) %reduce-scatter.2.cloned.1.call-update) | async-done | bytes 393232 | tf_op jit(solution)/shard_map/reduce_scatter | solution.py:49
  298.1 0.0 all-gather.6.cloned.1.call-update
  298.1 47.6 %all-gather.6.cloned.1.call-done = f32[384,2048]{1,0:T(8,128)} async-done(((f32[48,2048]{1,0:T(8,128)}), f32[384,2048]{1,0:T(8,128)}) %all-gather.6.cloned.1.call-update) | async-done | bytes 3145744 | tf_op jit(solution)/shard_map/all_gather | solution.py:11
  345.8 2.8 reduce_sum.9
  (1 shorter events, 0.0 us)
Async XLA Ops:
  6.5 100.4 %all-gather.4.cloned.1.call-start = ((), (), s32[]{:S(2)}) async-start(), calls=%async_computation.1 | async-start | bytes 6488064 | tf_op jit(solution)/shard_map/all_gather | solution.py:22
  7.3 290.9 %reduce-scatter.2.cloned.1.call-start = ((), (), s32[]{:S(2)}) async-start(), calls=%async_computation.2 | async-start | bytes 12976128 | tf_op jit(solution)/shard_map/reduce_scatter | solution.py:49
  107.0 5.6 %copy-start = (f32[2048]{0:T(1024)S(1)}, f32[2048]{0:T(1024)}, u32[]{:S(2)}) copy-start(f32[2048]{0:T(1024)} %param.7) | copy-start | bytes 24580
  112.6 3.7 %slice-start = ((s8[6291456]{0:T(1024)(128)(4,1)}), s8[4194304]{0:T(1024)(128)(4,1)S(1)}, s32[]{:S(2)}) async-start(s8[6291456]{0:T(1024)(128)(4,1)} %bitcast.12), calls=%async_computation.4 | async-start | bytes 8388608
  112.6 3.7 %slice-start.1 = ((s8[6291456]{0:T(1024)(128)(4,1)}), s8[2097152]{0:T(1024)(128)(4,1)S(1)}, s32[]{:S(2)}) async-start(s8[6291456]{0:T(1024)(128)(4,1)} %bitcast.12), calls=%async_computation.5 | async-start | bytes 4194304
  118.6 1.9 copy-start.1
  118.6 1.9 copy-start.2
  128.5 217.3 %all-gather.6.cloned.1.call-start = ((), (), s32[]{:S(2)}) async-start(), calls=%async_computation.3 | async-start | bytes 3538944 | tf_op jit(solution)/shard_map/all_gather | solution.py:11
Sparse Core Ops, SparseCore 0:
  10.1 96.7 all-gather.3
  128.6 169.4 reduce-scatter.1
  299.9 45.8 all-gather.5

commit v2 on v0

--- a/solution.py
+++ b/solution.py
@@ -7,6 +7,11 @@
 R1_WEIGHT = 40.0
 
 
+def all_by_exchange(x, name, dim):
+    outgoing = jnp.stack([x] * lax.axis_size(name))
+    return jnp.concatenate(lax.all_to_all(outgoing, name, 0, 0), axis=dim)
+
+
 def per_device(fake_tokens, real_tokens, proj_weight, score_vector):
     fake_rows = fake_tokens[0]
     real_rows = real_tokens[0]
@@ -14,7 +19,7 @@
     hid_width = proj_weight.shape[1]
     loss_scale = math.sqrt(hid_width / (lax.axis_size("grp") * lax.axis_size("seq") * tok_count))
     joined = jnp.concatenate([fake_rows, real_rows], 0)
-    shard_rows = lax.all_gather(proj_weight, "seq", axis=0, tiled=True)
+    shard_rows = all_by_exchange(proj_weight, "seq", 0)
     partial_pre = jnp.dot(joined, shard_rows, preferred_element_type=jnp.float32)
     full_weight = shard_rows
     preact, full_weight = (partial_pre, full_weight)

time: 388 us -> 439 us (1.13)
  blocking collectives: 0 us -> 152 us
  waiting for transfers between devices: 351 us -> 251 us
    all_to_all x0 -> x1, blocking collectives: none -> 152 us  [all_by_exchange(): return jnp.concatenate(lax.all_to_all(outgoing, name, 0, 0), axis=dim)]
    all_gather x1 -> x0, waiting for transfers between devices: 99.7 us -> none  [per_device(): shard_rows = lax.all_gather(proj_weight, 'seq', axis=0, tiled=True)]
  transfers between devices with their start and end apart: 3 -> 2, of which waited for: 3 -> 2; matrix products, arithmetic and copies ran while one was open for 0% -> 0% of each run, Pallas kernels for 0% -> 0%
where the time goes in v2:
time: 439 us
  waiting for transfers between devices  251 us (57%)
  blocking collectives  152 us (35%)
  matrix products  18.7 us (4%)
  between operations  13.5 us (3%)
    reduce_scatter x1, waiting for transfers between devices, per_device(): lax.psum_scatter(grad_term, 'seq', scatter_dimension=0, tiled=True)  170 us
    all_to_all x1, blocking collectives, all_by_exchange(): return jnp.concatenate(lax.all_to_all(outgoing, name, 0, 0), axis=dim)  152 us
    psum x1, waiting for transfers between devices, per_device(): return lax.psum(grad_shard, 'grp')  81.2 us
  transfers between devices with their start and end apart: 2, of which 2 were waited for; matrix products, arithmetic and copies ran while one was open for 0% of the time, Pallas kernels for 0%

profile of v2, /device:TPU:32, one launch (start us, length us, event | category | flops | bytes accessed | tf_op | source)
XLA Modules:
  0.0 439.1 jit_solution(9125207531550973211)
XLA Ops:
  6.5 0.0 reduce-scatter.2.cloned.1.call-start
  6.5 1.7 stack.2
  8.3 0.0 copy-start.1
  8.3 0.0 copy-start.2
  8.3 151.7 %all_to_all.5 = bf16[32,48,2048]{2,1,0:T(8,128)(2,1)S(1)} all-to-all(bf16[32,48,2048]{2,1,0:T(8,128)(2,1)S(1)} %stack.2), channel_id=1, replica_groups=mesh['grp'=8,'seq'=32] {'seq'}, dimensions={0} | all-to-all | bytes 12582912 | tf_op jit(solution)/shard_map/all_to_all | solution.py:12
  160.0 0.0 copy-done.1
  160.0 0.0 copy-done.2
  160.0 0.0 copy-start
  160.0 3.1 add_divide_fusion
  163.1 0.0 copy-done
  163.1 3.3 fusion.25
  166.4 0.1 divide_multiply_fusion.1
  166.5 0.3 fusion.20
  166.8 2.3 fusion.5
  169.1 1.9 fusion.4
  171.0 8.1 %fusion.6 = f32[1536,2048]{1,0:T(8,128)} fusion(bf16[192,2048]{1,0:T(8,128)(2,1)S(1)} %get-tuple-element.6, bf16[192,2048]{1,0:T(8,128)(2,1)S(1)} %fusion.4, bf16[192,2048]{1,0:T(8,128)(2,1)S(1)} %get-tuple-element.5, bf16[192,1536]{1,0:T(8,128)(2,1)S(1)} %fusion.5, bf16[192,1536]{1,0:T(8,128)(2,1)S(1)} %bitcast.15, bf16[192,1536]{1,0:T(8,128)(2,1)S(1)} %bitcast.17), kind=kOutput, calls=%fused_computation.10 | convolution fusion | flops 3636264960 | bytes 16711680 | tf_op jit(solution)/shard_map/dot_general | solution.py:46
  179.1 0.0 reduce-scatter.2.cloned.1.call-update
  179.1 0.0 all-reduce.2.cloned.1.call-start
  179.2 170.1 %reduce-scatter.2.cloned.1.call-done = f32[48,2048]{1,0:T(8,128)} async-done(((f32[1536,2048]{1,0:T(8,128)}), f32[48,2048]{1,0:T(8,128)}) %reduce-scatter.2.cloned.1.call-update) | async-done | bytes 393232 | tf_op jit(solution)/shard_map/reduce_scatter | solution.py:49
  349.2 0.0 all-reduce.2.cloned.1.call-update
  349.3 81.2 %all-reduce.2.cloned.1.call-done = f32[48,2048]{1,0:T(8,128)} async-done(((f32[48,2048]{1,0:T(8,128)}), f32[48,2048]{1,0:T(8,128)}) %all-reduce.2.cloned.1.call-update) | async-done | bytes 393232 | tf_op jit(solution)/shard_map/psum | solution.py:50
  430.5 1.8 copy.6
Async XLA Ops:
  6.5 342.7 %reduce-scatter.2.cloned.1.call-start = ((), (), s32[]{:S(2)}) async-start(), calls=%async_computation.2 | async-start | bytes 12976128 | tf_op jit(solution)/shard_map/reduce_scatter | solution.py:49
  8.3 151.7 %copy-start.1 = (bf16[1,192,1536]{2,1,0:T(8,128)(2,1)S(1)}, bf16[1,192,1536]{2,1,0:T(8,128)(2,1)}, u32[]{:S(2)}) copy-start(bf16[1,192,1536]{2,1,0:T(8,128)(2,1)} %param.5) | copy-start | bytes 1769476
  8.3 151.7 %copy-start.2 = (bf16[1,192,1536]{2,1,0:T(8,128)(2,1)S(1)}, bf16[1,192,1536]{2,1,0:T(8,128)(2,1)}, u32[]{:S(2)}) copy-start(bf16[1,192,1536]{2,1,0:T(8,128)(2,1)} %param.4) | copy-start | bytes 1769476
  160.0 3.1 copy-start
  179.1 251.4 %all-reduce.2.cloned.1.call-start = ((), (), s32[]{:S(2)}) async-start(), calls=%async_computation.3 | async-start | bytes 786432 | tf_op jit(solution)/shard_map/psum | solution.py:50
Sparse Core Ops, SparseCore 0:
  179.3 169.9 reduce-scatter.1
  351.9 78.6 all-reduce.1
